TPU v7x, 32 devices: a whole 2x2x4 slice. The times are simulated.
32 devices in a mesh: band: 8 (over z, x), rows: 4 (over y, core).
Axes of the slice: x: 2, y: 2, z: 4, core: 2. Of those that a mesh axis runs over, the one named last changes fastest.
Arguments:
- latents: bfloat16 [33280, 16], P(('band', 'rows')), may hold values from -6 to 6
- token_cell: int32 [33280], P(('band', 'rows')), may hold values from 0 to 33279, as said below
- frame_counts: int32 [8], replicated, may hold values from 1 to 4, 13 in all
- in_kernel: bfloat16 [3, 3, 3, 16, 384], replicated, may hold values from -0.3125 to 0.3125
- in_bias: float32 [384], replicated, may hold values from -3 to 3
- mid_kernel: bfloat16 [3, 3, 3, 384, 384], replicated, may hold values from -0.0625 to 0.0625
- mid_bias: float32 [384], replicated, may hold values from -3 to 3
Outputs:
- decoded: bfloat16 [32, 16, 160, 384], P('band', 'rows')
Inputs may be any that keep to these rules, and one draw needn't show every extreme that they name: `token_cell`: rows d * 1040 to (d + 1) * 1040 - 1 (d the flat index over band+rows) are, in some order, the cells f * 16 * 160 + d * 80 + s for every f < 13 and s < 80, each once. `frame_counts`: the counts sum to 13; some band holds 4 frames.
All inputs are finite; a program needn't handle non-finite values.
Results may differ from a plain program's by a relative error of at most 0.0043.
Values may be sent and summed in bfloat16 or wider, within the bound.
A program may use at most 64 MiB of HBM per device.

v0:
```python
import jax
import jax.numpy as jnp
from jax import lax
from jax.sharding import PartitionSpec as P

W = 160
R = 4
FCAP = 4


conv_layout = ("NDHWC", "DHWIO", "NDHWC")


def shifted(shard, axis, by):
    count = lax.axis_size(axis)
    pairs = [(i, i + by) for i in range(count) if 0 <= i + by < count]
    return lax.ppermute(shard, axis, pairs)


def extended_2(shard, sides, width):
    for axis, dim in sides:
        count, length = (lax.axis_size(axis), shard.shape[dim])
        up = [(i, (i + 1) % count) for i in range(count - 1)]
        down = [(j, i) for i, j in up]
        last = lax.slice_in_dim(shard, length - width, length, axis=dim)
        first = lax.slice_in_dim(shard, 0, width, axis=dim)
        before = lax.ppermute(last, axis, up)
        after = lax.ppermute(first, axis, down)
        shard = jnp.concatenate([before, shard, after], axis=dim)
    return shard


def convolve(frames, kernel):
    return lax.conv_general_dilated(
        frames[None],
        kernel,
        (1, 1, 1),
        [(0, 0), (0, 0), (1, 1)],
        dimension_numbers=conv_layout,
        preferred_element_type=jnp.float32,
    )[0]


def band_tables(frame_counts):
    ends = jnp.cumsum(frame_counts)
    return (ends - frame_counts, ends)


def right_tail(frames, own_count, depth):
    zeros_front = jnp.zeros((depth,) + frames.shape[1:], frames.dtype)
    joined = jnp.concatenate([zeros_front, frames], axis=0)
    return lax.dynamic_slice_in_dim(joined, own_count, depth, 0)


def assemble(received, frame_counts, depth):
    band_index = lax.axis_index("band")
    band_count = frame_counts.shape[0]
    starts, ends = band_tables(frame_counts)
    start_here = starts[band_index]
    pieces = []
    for offset in range(depth):
        frame_at = start_here - depth + offset
        chosen = jnp.zeros_like(received[0][0])
        for distance in range(1, depth + 1):
            owner_band = band_index - distance
            clipped = jnp.clip(owner_band, 0, band_count - 1)
            inside = (owner_band >= 0) & (frame_at >= starts[clipped]) & (frame_at < ends[clipped])
            position = jnp.clip(frame_at - ends[clipped] + depth, 0, depth - 1)
            candidate = lax.dynamic_index_in_dim(
                received[distance - 1], position, 0, keepdims=False
            )
            chosen = jnp.where(inside, candidate, chosen)
        pieces.append(chosen)
    return jnp.stack(pieces)


def per_device(latents, token_cell, frame_counts, in_kernel, in_bias, mid_kernel, mid_bias):
    band_total = lax.axis_size("band")
    rows_total = lax.axis_size("rows")
    band_index = lax.axis_index("band")
    rows_index = lax.axis_index("rows")
    channels = latents.shape[1]
    span_cells = R * W // band_total
    plane_cells = R * rows_total * W
    starts, ends = band_tables(frame_counts)
    frame_of = token_cell // plane_cells
    spot_index = token_cell % span_cells
    owners = jnp.sum((frame_of[:, None] >= ends[None, :]).astype(jnp.int32), axis=1)
    onehot = (owners[:, None] == jnp.arange(band_total, dtype=jnp.int32)[None, :]).astype(jnp.int32)
    slot_of = frame_of - jnp.sum(onehot * starts[None, :], axis=1)
    position = (owners * FCAP + slot_of) * span_cells + spot_index
    outgoing = (
        jnp.zeros((band_total * FCAP * span_cells, channels), latents.dtype)
        .at[position]
        .set(latents)
    )
    outgoing = outgoing.reshape(band_total, FCAP, span_cells * channels)
    target_rows = (band_index * rows_total + rows_index) // band_total
    spread = jnp.zeros((band_total, rows_total, FCAP, 1, span_cells * channels), latents.dtype)
    spread = lax.dynamic_update_slice_in_dim(spread, outgoing[:, None, :, None, :], target_rows, 1)
    spread = spread.reshape(band_total * rows_total, FCAP, 1, span_cells * channels)
    arrived = lax.all_to_all(spread, ("band", "rows"), split_axis=0, concat_axis=2, tiled=True)
    own_block = lax.dynamic_slice_in_dim(arrived, rows_index * band_total, band_total, 2)
    grid_local = own_block.reshape(FCAP, R, W * channels)
    own_count = frame_counts[band_index]
    tail_frames = right_tail(grid_local, own_count, 2)
    received = [shifted(tail_frames, "band", distance) for distance in range(1, 3)]
    extended = jnp.concatenate([assemble(received, frame_counts, 2), grid_local], axis=0)
    extended = extended_2(extended, (("rows", 1),), 1)
    first_conv = convolve(extended.reshape(FCAP + 2, R + 2, W, channels), in_kernel) + in_bias
    active = jax.nn.silu(first_conv).astype(jnp.bfloat16)
    tail_active = right_tail(active, own_count, 2)
    received_active = [shifted(tail_active, "band", distance) for distance in range(1, 3)]
    mixing_input = jnp.concatenate([assemble(received_active, frame_counts, 2), active], axis=0)
    mixing_input = extended_2(mixing_input, (("rows", 1),), 1)
    mixed = convolve(mixing_input, mid_kernel) + mid_bias
    live_slots = jnp.arange(FCAP, dtype=jnp.int32) < own_count
    decoded = jnp.where(live_slots[:, None, None, None], mixed, 0.0).astype(jnp.bfloat16)
    return decoded


def solution(mesh):
    placed = (P(("band", "rows"), None), P(("band", "rows")), P(), P(), P(), P(), P())
    return jax.shard_map(
        per_device,
        mesh=mesh,
        in_specs=placed,
        out_specs=P("band", "rows", None, None),
        check_vma=False,
    )
```

profile of v0, /device:TPU:11, one launch (start us, length us, event | category | flops | bytes accessed | tf_op | source)
XLA Modules:
  0.0 199.7 jit_solution(11292537899262426075)
XLA Ops:
  0.0 0.9 reduce-window.4
  0.9 0.7 bitcast_subtract_fusion
  1.5 0.7 add_select_fusion.1
  2.2 0.1 convert_reduce_fusion
  2.3 0.1 select_reduce_fusion
  2.4 0.7 compare_select_fusion
  3.1 0.9 copy.58
  4.1 6.3 %scatter_custom_fusion = bf16[2560,16]{1,0:T(8,128)(2,1)S(1)} fusion(s32[1040]{0:T(1024)S(1)} %compare_select_fusion, bf16[1040,16]{1,0:T(8,128)(2,1)S(1)} %copy.58, bf16[]{:T(256)} %constant.102.clone.1), kind=kCustom, calls=%fused_computation.33 | custom fusion | bytes 81922 | tf_op jit(solution)/shard_map/scatter | solution.py:95
  10.4 0.5 broadcast_in_dim_reshape.6
  10.9 0.8 broadcast_in_dim.17
  11.7 0.7 bitcast_dynamic-update-slice_fusion
  12.4 6.3 %all-to-all-start = ((bf16[32,4,1,1280]{3,1,2,0:T(4,128)(2,1)}), bf16[32,4,1,1280]{3,1,2,0:T(4,128)(2,1)S(1)}, u32[]{:S(2)}, u32[]{:S(2)}) async-start(bf16[32,4,1,1280]{3,1,2,0:T(4,128)(2,1)} %bitcast.8), calls=%async_computation | async-start | bytes 655360 | tf_op jit(solution)/shard_map/all_to_all | solution.py:102
  18.7 1.3 dynamic_slice.74
  21.9 6.9 %all-to-all-done = bf16[32,4,1,1280]{3,1,2,0:T(4,128)(2,1)S(1)} async-done(((bf16[32,4,1,1280]{3,1,2,0:T(4,128)(2,1)}), bf16[32,4,1,1280]{3,1,2,0:T(4,128)(2,1)S(1)}, u32[]{:S(2)}, u32[]{:S(2)}) %all-to-all-start) | async-done | bytes 327712 | tf_op jit(solution)/shard_map/all_to_all | solution.py:102
  28.8 0.1 reshape.40
  28.9 3.1 %collective-permute-start.1 = (bf16[2,4,2560]{2,1,0:T(4,128)(2,1)S(1)}, bf16[2,4,2560]{2,1,0:T(4,128)(2,1)S(1)}, u32[]{:S(2)}, u32[]{:S(2)}) collective-permute-start(bf16[2,4,2560]{2,1,0:T(4,128)(2,1)S(1)} %pad_dynamic-slice_fusion.1), channel_id=1, source_target_pairs={{0,4},{4,8},{8,12},{12,16},{16,20},{20,24},{24,28},{1,5},{5,9},{9,... | collective-permute-start | bytes 122888 | tf_op jit(solution)/shard_map/ppermute | solution.py:17
  32.0 2.3 %collective-permute-start = (bf16[2,4,2560]{2,1,0:T(4,128)(2,1)S(1)}, bf16[2,4,2560]{2,1,0:T(4,128)(2,1)S(1)}, u32[]{:S(2)}, u32[]{:S(2)}) collective-permute-start(bf16[2,4,2560]{2,1,0:T(4,128)(2,1)S(1)} %pad_dynamic-slice_fusion.1), channel_id=1, source_target_pairs={{0,8},{4,12},{8,16},{12,20},{16,24},{20,28},{1,9},{5,13},{9,17},{1... | collective-permute-start | bytes 122888 | tf_op jit(solution)/shard_map/ppermute | solution.py:17
  34.3 0.6 fusion.37
  38.6 0.6 constant_dynamic-slice_fusion.2
  44.1 0.0 collective-permute-done.1
  44.1 0.0 collective-permute-done
  44.2 0.1 pad_maximum_fusion.2
  44.3 0.1 fusion.36
  44.4 3.5 %collective-permute-start.2 = (bf16[6,1,2560]{2,1,0:T(2,128)(2,1)S(1)}, bf16[6,1,2560]{2,1,0:T(2,128)(2,1)S(1)}, u32[]{:S(2)}, u32[]{:S(2)}) collective-permute-start(bf16[6,1,2560]{2,1,0:T(2,128)(2,1)S(1)} %get-tuple-element.9), channel_id=1, source_target_pairs={{0,1},{1,2},{2,3},{4,5},{5,6},{6,7},{8,9},{9,10},{10,11},{12,13},{... | collective-permute-start | bytes 92168 | tf_op jit(solution)/shard_map/ppermute | solution.py:27
  47.9 2.2 %collective-permute-start.3 = (bf16[6,1,2560]{2,1,0:T(2,128)(2,1)S(1)}, bf16[6,1,2560]{2,1,0:T(2,128)(2,1)S(1)}, u32[]{:S(2)}, u32[]{:S(2)}) collective-permute-start(bf16[6,1,2560]{2,1,0:T(2,128)(2,1)S(1)} %get-tuple-element.10), channel_id=1, source_target_pairs={{1,0},{2,1},{3,2},{5,4},{6,5},{7,6},{9,8},{10,9},{11,10},{13,12},{... | collective-permute-start | bytes 92168 | tf_op jit(solution)/shard_map/ppermute | solution.py:28
  50.1 0.0 collective-permute-done.2
  50.1 3.3 %collective-permute-done.3 = bf16[6,1,2560]{2,1,0:T(2,128)(2,1)S(1)} collective-permute-done((bf16[6,1,2560]{2,1,0:T(2,128)(2,1)S(1)}, bf16[6,1,2560]{2,1,0:T(2,128)(2,1)S(1)}, u32[]{:S(2)}, u32[]{:S(2)}) %collective-permute-start.3) | collective-permute-done | bytes 30752 | tf_op jit(solution)/shard_map/ppermute | solution.py:28
  53.4 0.2 pad_maximum_fusion.1
  53.6 1.2 reshape.55
  54.8 1.6 pad.2
  56.4 2.4 %reshape.78 = bf16[6,6,1,8,21,16]{5,4,3,1,0,2:T(8,128)(2,1)S(1)} reshape(bf16[6,6,1,168,16]{4,3,1,0,2:T(8,128)(2,1)} %pad.2) | data formatting | bytes 387072 | tf_op jit(solution)/shard_map/conv_general_dilated | solution.py:34
  58.9 0.2 copy.64
  59.1 0.0 copy-done
  59.1 0.0 copy-done.4
  59.1 3.5 %broadcast_select_fusion = f32[4,4,8,21,384]{4,2,3,1,0:T(8,128)S(1)} fusion(pred[8,21]{0,1:T(8,128)(4,1)S(1)} %copy-done.4, bf16[3,3,3,16,384]{4,3,2,1,0:T(8,128)(2,1)S(1)} %copy-done, bf16[6,6,1,7,2,16]{5,3,4,1,0,2:T(8,128)(2,1)S(1)} %slice.22, bf16[6,6,1,8,21,16]{5,3,4,1,0,2:T(8,128)(2,1)S(1)} %copy.64), kind=kOutput, calls=%fused_computation.24 | convolution fusion | flops 893481984 | bytes 4670376 | tf_op jit(solution)/shard_map/conv_general_dilated | solution.py:34
  62.7 1.1 copy.65
  63.7 2.1 %fusion.12 = bf16[4,4,160,384]{3,1,2,0:T(4,128)(2,1)S(1)} fusion(f32[4,4,1,168,384]{4,1,3,0,2:T(4,128)S(1)} %bitcast.62, f32[384]{0:T(512)S(1)} %copy-done.2), kind=kLoop, calls=%fused_computation.17 | loop fusion | flops 5898240 | bytes 5899776 | tf_op jit(solution)/shard_map/convert_element_type | solution.py:111
  65.8 0.5 pad_dynamic-slice_fusion
  66.4 3.0 %collective-permute-start.5 = (bf16[2,4,160,384]{3,1,2,0:T(4,128)(2,1)S(1)}, bf16[2,4,160,384]{3,1,2,0:T(4,128)(2,1)S(1)}, u32[]{:S(2)}, u32[]{:S(2)}) collective-permute-start(bf16[2,4,160,384]{3,1,2,0:T(4,128)(2,1)S(1)} %pad_dynamic-slice_fusion), channel_id=1, source_target_pairs={{0,4},{4,8},{8,12},{12,16},{16,20},{20,24},{24,28},{1,5},{5,9},{9,... | collective-permute-start | bytes 2949128 | tf_op jit(solution)/shard_map/ppermute | solution.py:17
  69.3 1.9 collective-permute-start.4
  71.3 19.7 %collective-permute-done.5 = bf16[2,4,160,384]{3,1,2,0:T(4,128)(2,1)S(1)} collective-permute-done((bf16[2,4,160,384]{3,1,2,0:T(4,128)(2,1)S(1)}, bf16[2,4,160,384]{3,1,2,0:T(4,128)(2,1)S(1)}, u32[]{:S(2)}, u32[]{:S(2)}) %collective-permute-start.5) | collective-permute-done | bytes 983072 | tf_op jit(solution)/shard_map/ppermute | solution.py:17
  91.0 19.6 %collective-permute-done.4 = bf16[2,4,160,384]{3,1,2,0:T(4,128)(2,1)S(1)} collective-permute-done((bf16[2,4,160,384]{3,1,2,0:T(4,128)(2,1)S(1)}, bf16[2,4,160,384]{3,1,2,0:T(4,128)(2,1)S(1)}, u32[]{:S(2)}, u32[]{:S(2)}) %collective-permute-start.4) | collective-permute-done | bytes 983072 | tf_op jit(solution)/shard_map/ppermute | solution.py:17
  110.5 0.6 select_select_fusion.1
  111.1 2.1 %pad_maximum_fusion = bf16[6,4,160,384]{3,1,2,0:T(4,128)(2,1)S(1)} fusion(bf16[4,4,160,384]{3,1,2,0:T(4,128)(2,1)S(1)} %fusion.12, bf16[1,4,160,384]{3,1,2,0:T(4,128)(2,1)S(1)} %get-tuple-element.8, bf16[1,4,160,384]{3,1,2,0:T(4,128)(2,1)S(1)} %get-tuple-element.7), kind=kLoop, calls=%fused_computation.20 | loop fusion | flops 2949120 | bytes 5898240 | tf_op jit(solution)/shard_map/concatenate | solution.py:114
  113.2 2.1 %fusion.35 = (bf16[6,1,160,384]{3,1,2,0:T(2,128)(2,1)S(1)}, bf16[6,1,160,384]{3,1,2,0:T(2,128)(2,1)S(1)}) fusion(bf16[6,4,160,384]{3,1,2,0:T(4,128)(2,1)S(1)} %pad_maximum_fusion), kind=kLoop, calls=%fused_computation.63 | loop fusion | bytes 2949120 | tf_op jit(solution)/shard_map/slice | solution.py:25
  115.3 0.1 copy.67
  115.4 1.9 collective-permute-start.7
  117.4 0.1 copy.66
  117.5 19.8 %collective-permute-start.6 = (bf16[6,1,160,384]{3,2,1,0:T(8,128)(2,1)S(1)}, bf16[6,1,160,384]{3,2,1,0:T(8,128)(2,1)S(1)}, u32[]{:S(2)}, u32[]{:S(2)}) collective-permute-start(bf16[6,1,160,384]{3,2,1,0:T(8,128)(2,1)S(1)} %copy.66), channel_id=1, source_target_pairs={{0,1},{1,2},{2,3},{4,5},{5,6},{6,7},{8,9},{9,10},{10,11},{12,13},{... | collective-permute-start | bytes 2211848 | tf_op jit(solution)/shard_map/ppermute | solution.py:27
  137.3 0.6 iota_compare_fusion.3
  137.9 0.0 collective-permute-done.7
  137.9 1.1 copy.69
  139.1 0.0 collective-permute-done.6
  139.1 1.1 copy.68
  140.2 5.5 %maximum_bitcast_fusion = bf16[6,6,1,160,384]{4,1,3,0,2:T(8,128)(2,1)S(1)} fusion(bf16[6,1,160,384]{3,1,2,0:T(2,128)(2,1)S(1)} %copy.69, bf16[4,4,160,384]{3,1,2,0:T(4,128)(2,1)S(1)} %fusion.12, bf16[1,4,160,384]{3,1,2,0:T(4,128)(2,1)S(1)} %get-tuple-element.8, bf16[1,4,160,384]{3,1,2,0:T(4,128)(2,1)S(1)} %get-tuple-element.7, ...), kind=kLoop, calls=%fused_computation.3 | loop fusion | flops 22118400 | bytes 8847360 | tf_op jit(solution)/shard_map/broadcast_in_dim | solution.py:35
  145.7 1.0 pad.4
  146.7 0.6 copy.72
  147.3 0.1 slice.26
  147.5 48.5 %fusion.15 = f32[4,4,8,21,384]{4,2,3,1,0:T(8,128)S(1)} fusion(bf16[3,3,3,384,384]{4,3,2,1,0:T(8,128)(2,1)} %param.12, bf16[6,6,1,7,2,384]{5,3,4,1,0,2:T(8,128)(2,1)S(1)} %slice.26, bf16[6,6,1,8,21,384]{5,3,4,1,0,2:T(8,128)(2,1)S(1)} %copy.72, pred[8,21]{0,1:T(8,128)(4,1)S(1)} %copy-done.4), kind=kOutput, calls=%fused_computation.23 | convolution fusion | flops 21419827200 | bytes 17123496 | tf_op jit(solution)/shard_map/conv_general_dilated | solution.py:34
  196.0 0.0 copy-start.3
  196.0 1.1 copy.73
  197.1 0.0 copy-start.1
  197.1 0.9 fusion.10
  198.0 1.5 copy.74
  (11 shorter events, 0.2 us)
Async XLA Ops:
  0.0 59.1 %copy-start = (bf16[3,3,3,16,384]{4,3,2,1,0:T(8,128)(2,1)S(1)}, bf16[3,3,3,16,384]{4,3,2,1,0:T(8,128)(2,1)}, u32[]{:S(2)}) copy-start(bf16[3,3,3,16,384]{4,3,2,1,0:T(8,128)(2,1)} %param.10) | copy-start | bytes 995332
  12.4 16.4 %all-to-all-start = ((bf16[32,4,1,1280]{3,1,2,0:T(4,128)(2,1)}), bf16[32,4,1,1280]{3,1,2,0:T(4,128)(2,1)S(1)}, u32[]{:S(2)}, u32[]{:S(2)}) async-start(bf16[32,4,1,1280]{3,1,2,0:T(4,128)(2,1)} %bitcast.8), calls=%async_computation | async-start | bytes 655360 | tf_op jit(solution)/shard_map/all_to_all | solution.py:102
  28.9 15.2 %collective-permute-start.1 = (bf16[2,4,2560]{2,1,0:T(4,128)(2,1)S(1)}, bf16[2,4,2560]{2,1,0:T(4,128)(2,1)S(1)}, u32[]{:S(2)}, u32[]{:S(2)}) collective-permute-start(bf16[2,4,2560]{2,1,0:T(4,128)(2,1)S(1)} %pad_dynamic-slice_fusion.1), channel_id=1, source_target_pairs={{0,4},{4,8},{8,12},{12,16},{16,20},{20,24},{24,28},{1,5},{5,9},{9,... | collective-permute-start | bytes 122888 | tf_op jit(solution)/shard_map/ppermute | solution.py:17
  32.0 12.1 %collective-permute-start = (bf16[2,4,2560]{2,1,0:T(4,128)(2,1)S(1)}, bf16[2,4,2560]{2,1,0:T(4,128)(2,1)S(1)}, u32[]{:S(2)}, u32[]{:S(2)}) collective-permute-start(bf16[2,4,2560]{2,1,0:T(4,128)(2,1)S(1)} %pad_dynamic-slice_fusion.1), channel_id=1, source_target_pairs={{0,8},{4,12},{8,16},{12,20},{16,24},{20,28},{1,9},{5,13},{9,17},{1... | collective-permute-start | bytes 122888 | tf_op jit(solution)/shard_map/ppermute | solution.py:17
  44.4 5.7 %collective-permute-start.2 = (bf16[6,1,2560]{2,1,0:T(2,128)(2,1)S(1)}, bf16[6,1,2560]{2,1,0:T(2,128)(2,1)S(1)}, u32[]{:S(2)}, u32[]{:S(2)}) collective-permute-start(bf16[6,1,2560]{2,1,0:T(2,128)(2,1)S(1)} %get-tuple-element.9), channel_id=1, source_target_pairs={{0,1},{1,2},{2,3},{4,5},{5,6},{6,7},{8,9},{9,10},{10,11},{12,13},{... | collective-permute-start | bytes 92168 | tf_op jit(solution)/shard_map/ppermute | solution.py:27
  47.9 5.5 %collective-permute-start.3 = (bf16[6,1,2560]{2,1,0:T(2,128)(2,1)S(1)}, bf16[6,1,2560]{2,1,0:T(2,128)(2,1)S(1)}, u32[]{:S(2)}, u32[]{:S(2)}) collective-permute-start(bf16[6,1,2560]{2,1,0:T(2,128)(2,1)S(1)} %get-tuple-element.10), channel_id=1, source_target_pairs={{1,0},{2,1},{3,2},{5,4},{6,5},{7,6},{9,8},{10,9},{11,10},{13,12},{... | collective-permute-start | bytes 92168 | tf_op jit(solution)/shard_map/ppermute | solution.py:28
  56.4 2.7 %copy-start.4 = (pred[8,21]{0,1:T(8,128)(4,1)S(1)}, pred[8,21]{0,1:T(8,128)(4,1)}, u32[]{:S(2)}) copy-start(pred[8,21]{0,1:T(8,128)(4,1)} %constant.130) | copy-start | bytes 508
  62.6 1.1 copy-start.2
  66.4 24.6 %collective-permute-start.5 = (bf16[2,4,160,384]{3,1,2,0:T(4,128)(2,1)S(1)}, bf16[2,4,160,384]{3,1,2,0:T(4,128)(2,1)S(1)}, u32[]{:S(2)}, u32[]{:S(2)}) collective-permute-start(bf16[2,4,160,384]{3,1,2,0:T(4,128)(2,1)S(1)} %pad_dynamic-slice_fusion), channel_id=1, source_target_pairs={{0,4},{4,8},{8,12},{12,16},{16,20},{20,24},{24,28},{1,5},{5,9},{9,... | collective-permute-start | bytes 2949128 | tf_op jit(solution)/shard_map/ppermute | solution.py:17
  69.3 41.2 %collective-permute-start.4 = (bf16[2,4,160,384]{3,1,2,0:T(4,128)(2,1)S(1)}, bf16[2,4,160,384]{3,1,2,0:T(4,128)(2,1)S(1)}, u32[]{:S(2)}, u32[]{:S(2)}) collective-permute-start(bf16[2,4,160,384]{3,1,2,0:T(4,128)(2,1)S(1)} %pad_dynamic-slice_fusion), channel_id=1, source_target_pairs={{0,8},{4,12},{8,16},{12,20},{16,24},{20,28},{1,9},{5,13},{9,17},{1... | collective-permute-start | bytes 2949128 | tf_op jit(solution)/shard_map/ppermute | solution.py:17
  115.4 22.5 %collective-permute-start.7 = (bf16[6,1,160,384]{3,2,1,0:T(8,128)(2,1)S(1)}, bf16[6,1,160,384]{3,2,1,0:T(8,128)(2,1)S(1)}, u32[]{:S(2)}, u32[]{:S(2)}) collective-permute-start(bf16[6,1,160,384]{3,2,1,0:T(8,128)(2,1)S(1)} %copy.67), channel_id=1, source_target_pairs={{1,0},{2,1},{3,2},{5,4},{6,5},{7,6},{9,8},{10,9},{11,10},{13,12},{... | collective-permute-start | bytes 2211848 | tf_op jit(solution)/shard_map/ppermute | solution.py:28
  117.5 21.6 %collective-permute-start.6 = (bf16[6,1,160,384]{3,2,1,0:T(8,128)(2,1)S(1)}, bf16[6,1,160,384]{3,2,1,0:T(8,128)(2,1)S(1)}, u32[]{:S(2)}, u32[]{:S(2)}) collective-permute-start(bf16[6,1,160,384]{3,2,1,0:T(8,128)(2,1)S(1)} %copy.66), channel_id=1, source_target_pairs={{0,1},{1,2},{2,3},{4,5},{5,6},{6,7},{8,9},{9,10},{10,11},{12,13},{... | collective-permute-start | bytes 2211848 | tf_op jit(solution)/shard_map/ppermute | solution.py:27
  196.0 1.1 copy-start.3
  197.1 2.5 %copy-start.1 = (bf16[3,3,3,16,384]{4,3,2,1,0:T(8,128)(2,1)S(1)}, bf16[3,3,3,16,384]{4,3,2,1,0:T(8,128)(2,1)}, u32[]{:S(2)}) copy-start(bf16[3,3,3,16,384]{4,3,2,1,0:T(8,128)(2,1)} %param.10) | copy-start | bytes 995332
where the time goes:
time: 200 us
  matrix products  52 us (26%)
  waiting for transfers between devices  49.5 us (25%)
  starting transfers between devices  43.9 us (22%)
  local copies, waits for them, and re-layouts  28 us (14%)
  other arithmetic  15.2 us (8%)
  between operations  11.1 us (6%)
    conv_general_dilated x2, matrix products, convolve(): lax.conv_general_dilated(frames[None], kernel, (1, 1, 1), [(0, 0), (0, 0)...  52 us
    ppermute x4, waiting for transfers between devices, shifted(): return lax.ppermute(shard, axis, pairs)  39.3 us
    ppermute x2, starting transfers between devices, extended_2(): before = lax.ppermute(last, axis, up)  23.3 us
    ppermute x4, starting transfers between devices, shifted(): return lax.ppermute(shard, axis, pairs)  10.2 us
    all_to_all x1, waiting for transfers between devices, per_device(): lax.all_to_all(spread, ('band', 'rows'), split_axis=0, concat_axis=2, til...  6.86 us
    all_to_all x1, starting transfers between devices, per_device(): lax.all_to_all(spread, ('band', 'rows'), split_axis=0, concat_axis=2, til...  6.33 us
    scatter x1, local copies, waits for them, and re-layouts, per_device(): outgoing = jnp.zeros((band_total * FCAP * span_cells, channels), latents....  6.29 us
    conv_general_dilated x7, local copies, waits for them, and re-layouts, convolve(): lax.conv_general_dilated(frames[None], kernel, (1, 1, 1), [(0, 0), (0, 0)...  5.5 us
  transfers between devices with their start and end apart: 9, of which 4 were waited for; matrix products, arithmetic and copies ran while one was open for 2% of the time, Pallas kernels for 0%

commit v1 on v0

v1 whole, which is shorter than its diff:
```python
import functools

import jax
import jax.numpy as jnp
from jax import lax
from jax.experimental import pallas as pl
from jax.experimental.pallas import tpu as pltpu
from jax.sharding import PartitionSpec as P

W = 160
R = 4
FCAP = 4
BACK = 2
IN_FRAMES = FCAP + 2 * BACK
IN_ROWS = R + 4
MID_FRAMES = FCAP + BACK
MID_ROWS = R + 2
LANES = 128
MESH = pl.DeviceIdType.MESH


def exchange_kernel(bands, rows, counts, lat, cell, out, store, send, recv, send_sem, recv_sem):
    n, channels = lat.shape
    span = R * W // bands
    parts = W // span
    frames = n // span
    plane = R * rows * W
    band = lax.axis_index("band")
    row = lax.axis_index("rows")
    me = band * rows + row
    y = lax.div(me, parts)
    part = lax.rem(me, parts)
    home = lax.div(y, R)
    y_in = lax.rem(y, R)
    near = jnp.where(y_in < 2, home - 1, home + 1)
    near_ok = (near >= 0) & (near < rows)
    slot_home = (y_in + 2) * parts + part
    slot_near = jnp.where(y_in < 2, y_in + 6, y_in - 2) * parts + part

    def source(slot):
        src_y = R * row - 2 + slot // parts
        src = src_y * parts + slot % parts
        ok = (src_y >= 0) & (src_y < R * rows) & (src != me)
        src = jnp.maximum(src, 0)
        return lax.div(src, rows), lax.rem(src, rows), ok

    barrier = pltpu.get_barrier_semaphore()
    for slot in range(IN_ROWS * parts):
        src_band, src_row, ok = source(slot)

        @pl.when(ok)
        def _():
            pl.semaphore_signal(barrier, inc=1, device_id=(src_band, src_row), device_id_type=MESH)

    cells = cell[...]
    frame = jnp.zeros_like(cells)
    for f in range(1, frames):
        frame = frame + (cells >= f * plane).astype(jnp.int32)
    lane_of = cells - frame * plane - me * span + part * span + 1
    lane_of = jnp.where(lane_of >= LANES, lane_of - LANES, lane_of)
    eye = (
        lax.broadcasted_iota(jnp.int32, (channels, channels), 0)
        == lax.broadcasted_iota(jnp.int32, (channels, channels), 1)
    )
    eye = jnp.where(eye, 1.0, 0.0).astype(jnp.bfloat16)
    across = (((1,), (1,)), ((), ()))
    lat_t = lax.dot_general(eye, lat[...], across, preferred_element_type=jnp.float32)
    by_frame = jnp.concatenate(
        [jnp.where(frame == f, lat_t, 0.0).astype(jnp.bfloat16) for f in range(frames)], axis=0
    )
    spot = lax.broadcasted_iota(jnp.int32, (LANES, n), 0) == lane_of
    spot = jnp.where(spot, 1.0, 0.0).astype(jnp.bfloat16)
    placed = lax.dot_general(by_frame, spot, across, preferred_element_type=jnp.float32)
    store[:FCAP] = jnp.zeros((FCAP, channels, LANES), jnp.bfloat16)
    store[FCAP + frames:] = jnp.zeros((FCAP, channels, LANES), jnp.bfloat16)
    store[FCAP:FCAP + frames] = placed.astype(jnp.bfloat16).reshape(frames, channels, LANES)

    here = (home == row).astype(jnp.int32) + (near == row).astype(jnp.int32)
    total = bands + jnp.where(near_ok, bands, 0) - here
    pl.semaphore_wait(barrier, total)

    def copy_to(i, target, which, slot):
        to_band = lax.rem(band + i, bands)
        return pltpu.make_async_remote_copy(
            src_ref=send.at[i],
            dst_ref=recv.at[slot],
            send_sem=send_sem.at[which, i],
            recv_sem=recv_sem.at[slot],
            device_id=(to_band, target),
            device_id_type=MESH,
        )

    for i in range(bands):
        to_band = lax.rem(band + i, bands)
        start = jnp.int32(0)
        for q in range(bands - 1):
            start = start + jnp.where(q < to_band, counts[q], 0)
        for j in range(IN_FRAMES):
            send[i, j] = store[start + j]
        for which, target, slot, ok in ((0, home, slot_home, None), (1, near, slot_near, near_ok)):
            away = jnp.bool_(True) if i else target != row
            go = away if ok is None else away & ok

            @pl.when(go)
            def _():
                copy_to(i, target, which, slot).start()

            if i == 0:
                @pl.when(target == row)
                def _():
                    recv[slot] = send[0]

    for slot in range(IN_ROWS * parts):
        src_band, src_row, ok = source(slot)

        @pl.when(ok)
        def _():
            pltpu.make_async_remote_copy(
                src_ref=send.at[0],
                dst_ref=recv.at[slot],
                send_sem=send_sem.at[0, 0],
                recv_sem=recv_sem.at[slot],
                device_id=(src_band, src_row),
                device_id_type=MESH,
            ).wait_recv()

    lane = lax.broadcasted_iota(jnp.int32, (IN_FRAMES, channels, LANES), 2)
    for yy in range(IN_ROWS):
        at = R * row - 2 + yy
        inside = (at >= 0) & (at < R * rows)

        @pl.when(inside)
        def _():
            low = recv[yy * parts].astype(jnp.float32)
            for p in range(1, parts):
                piece = recv[yy * parts + p].astype(jnp.float32)
                low = jnp.where(lane >= p * span + 1, piece, low)
            high = jnp.where(lane < W + 1 - LANES, piece, 0.0)
            out[yy, :, :, :LANES] = low.astype(jnp.bfloat16)
            out[yy, :, :, LANES:] = high.astype(jnp.bfloat16)

        @pl.when(jnp.logical_not(inside))
        def _():
            out[yy] = jnp.zeros(out.shape[1:], jnp.bfloat16)

    for i in range(bands):
        for which, target, slot, ok in ((0, home, slot_home, None), (1, near, slot_near, near_ok)):
            away = jnp.bool_(True) if i else target != row
            go = away if ok is None else away & ok

            @pl.when(go)
            def _():
                copy_to(i, target, which, slot).wait_send()


def conv_kernel(bands, rows, counts, xin, w1, b1, w2, b2, out, xs, mid, wcat, acc, obuf, w_sem, o_sem):
    channels = xin.shape[2]
    wide = w1.shape[1]
    depth = 3 * wide
    band = lax.axis_index("band")
    row = lax.axis_index("rows")

    def weight_copy(a, b):
        return pltpu.make_async_copy(
            w2.at[a, b], wcat.at[b, :, pl.ds((2 - a) * wide, wide)], w_sem.at[a, b]
        )

    for b in range(3):
        for a in range(3):
            weight_copy(a, b).start()

    start = jnp.int32(0)
    for q in range(bands - 1):
        start = start + jnp.where(q < band, counts[q], 0)
    own = counts[band]

    def shift_row(yy, carry):
        whole = xin[yy].astype(jnp.float32)
        flat = whole.reshape(IN_FRAMES * channels, 2 * LANES)
        for e in range(3):
            moved = flat if e == 0 else pltpu.roll(flat, 2 * LANES - e, 1)
            moved = moved[:, :W].astype(jnp.bfloat16)
            xs[e, yy] = moved.reshape(IN_FRAMES, channels, W)
        return carry

    lax.fori_loop(0, IN_ROWS, shift_row, 0)

    place = lax.broadcasted_iota(jnp.int32, (W, wide), 0)

    def first(i, carry):
        f = lax.div(i, MID_ROWS)
        y = lax.rem(i, MID_ROWS)
        taps = [xs[e, y + b, f + a] for a in range(3) for b in range(3) for e in range(3)]
        lhs = jnp.concatenate(taps, axis=0)
        v = lax.dot_general(
            lhs, w1[...], (((0,), (0,)), ((), ())), preferred_element_type=jnp.float32
        )
        v = v + b1[...]
        at = R * row - 1 + y
        inside = (at >= 0) & (at < R * rows) & (start - BACK + f >= 0)
        half = 0.5 * v
        active = jnp.where(inside, half * jnp.tanh(half) + half, 0.0)
        before = jnp.where(place == 0, 0.0, pltpu.roll(active, 1, 0))
        after = jnp.where(place == W - 1, 0.0, pltpu.roll(active, W - 1, 0))
        mid[f, y, :, :wide] = before.astype(jnp.bfloat16)
        mid[f, y, :, wide:2 * wide] = active.astype(jnp.bfloat16)
        mid[f, y, :, 2 * wide:] = after.astype(jnp.bfloat16)
        return carry

    lax.fori_loop(0, MID_FRAMES * MID_ROWS, first, 0)

    for b in range(3):
        for a in range(3):
            weight_copy(a, b).wait()

    for pair in range(FCAP // 2):
        acc[...] = jnp.broadcast_to(b2[...], acc.shape)

        def taps_of(b, carry):
            def rows_of(g):
                return mid[2 * pair + g, pl.ds(b, R)].reshape(R * W, depth)

            acc[:, :wide] += jnp.dot(
                rows_of(0), wcat[b, :, 2 * wide:], preferred_element_type=jnp.float32
            )
            acc[...] += jnp.dot(
                rows_of(1), wcat[b, :, wide:], preferred_element_type=jnp.float32
            )
            acc[...] += jnp.dot(
                rows_of(2), wcat[b, :, :2 * wide], preferred_element_type=jnp.float32
            )
            acc[:, wide:] += jnp.dot(
                rows_of(3), wcat[b, :, :wide], preferred_element_type=jnp.float32
            )
            return carry

        lax.fori_loop(0, 3, taps_of, 0)
        for k in range(2):
            t = 2 * pair + k
            value = acc[:, k * wide:(k + 1) * wide]
            value = jnp.where(t < own, value, 0.0).astype(jnp.bfloat16)
            obuf[t] = value.reshape(R, W, wide)
            pltpu.make_async_copy(obuf.at[t], out.at[t], o_sem.at[t]).start()
    for t in range(FCAP):
        pltpu.make_async_copy(obuf.at[t], out.at[t], o_sem.at[t]).wait()


def per_device(bands, rows, latents, token_cell, frame_counts, in_kernel, in_bias, mid_kernel, mid_bias):
    n, channels = latents.shape
    wide = in_kernel.shape[-1]
    span = R * W // bands
    parts = W // span
    frames = n // span
    vmem = pl.BlockSpec(memory_space=pltpu.VMEM)
    smem = pl.BlockSpec(memory_space=pltpu.SMEM)
    anywhere = pl.BlockSpec(memory_space=pl.ANY)
    tile = (IN_FRAMES, channels, LANES)
    xin = pl.pallas_call(
        functools.partial(exchange_kernel, bands, rows),
        out_shape=jax.ShapeDtypeStruct((IN_ROWS, IN_FRAMES, channels, 2 * LANES), jnp.bfloat16),
        in_specs=[smem, vmem, vmem],
        out_specs=vmem,
        scratch_shapes=[
            pltpu.VMEM((frames + 2 * FCAP, channels, LANES), jnp.bfloat16),
            pltpu.VMEM((bands,) + tile, jnp.bfloat16),
            pltpu.VMEM((IN_ROWS * parts,) + tile, jnp.bfloat16),
            pltpu.SemaphoreType.DMA((2, bands)),
            pltpu.SemaphoreType.DMA((IN_ROWS * parts,)),
        ],
        compiler_params=pltpu.CompilerParams(
            collective_id=0, has_side_effects=True, vmem_limit_bytes=32 * 1024 * 1024
        ),
        name="exchange",
    )(frame_counts, latents, token_cell.reshape(1, n))
    flops = 2 * FCAP * R * W * 27 * wide * wide
    return pl.pallas_call(
        functools.partial(conv_kernel, bands, rows),
        out_shape=jax.ShapeDtypeStruct((FCAP, R, W, wide), jnp.bfloat16),
        in_specs=[smem, vmem, vmem, vmem, anywhere, vmem],
        out_specs=anywhere,
        scratch_shapes=[
            pltpu.VMEM((3, IN_ROWS, IN_FRAMES, channels, W), jnp.bfloat16),
            pltpu.VMEM((MID_FRAMES, MID_ROWS, W, 3 * wide), jnp.bfloat16),
            pltpu.VMEM((3, 3 * wide, 3 * wide), jnp.bfloat16),
            pltpu.VMEM((R * W, 2 * wide), jnp.float32),
            pltpu.VMEM((FCAP, R, W, wide), jnp.bfloat16),
            pltpu.SemaphoreType.DMA((3, 3)),
            pltpu.SemaphoreType.DMA((FCAP,)),
        ],
        compiler_params=pltpu.CompilerParams(vmem_limit_bytes=56 * 1024 * 1024),
        cost_estimate=pl.CostEstimate(flops=flops, bytes_accessed=12 << 20, transcendentals=0),
        name="convs",
    )(
        frame_counts,
        xin,
        in_kernel.reshape(27 * channels, wide),
        in_bias.reshape(1, wide),
        mid_kernel.reshape(3, 3, 3 * wide, wide),
        jnp.concatenate([mid_bias, mid_bias]).reshape(1, 2 * wide),
    )


def solution(mesh):
    placed = (P(("band", "rows"), None), P(("band", "rows")), P(), P(), P(), P(), P())
    return jax.shard_map(
        functools.partial(per_device, mesh.shape["band"], mesh.shape["rows"]),
        mesh=mesh,
        in_specs=placed,
        out_specs=P("band", "rows", None, None),
        check_vma=False,
    )
```

time: 200 us -> 67 us (0.34)
  Pallas kernels: 0 us -> 61.1 us
  matrix products: 52 us -> 0 us
  waiting for transfers between devices: 49.5 us -> 0 us
  starting transfers between devices: 43.9 us -> 0 us
  local copies, waits for them, and re-layouts: 28 us -> 4.88 us
  other arithmetic: 15.2 us -> 0.76 us
  between operations: 11.1 us -> 0.04 us
    pallas_call x0 -> x2, Pallas kernels: none -> 61.1 us  [the longest x1 42.6 us: per_device(): pl.pallas_call(functools.partial(conv_kernel, bands, rows), out_shape=jax...]
    conv_general_dilated x2 -> x0, matrix products: 52 us -> none  [convolve(): lax.conv_general_dilated(frames[None], kernel, (1, 1, 1), [(0, 0), (0, 0)...]
    ppermute x8 -> x0, waiting for transfers between devices: 42.6 us -> none  [the longest x4 39.3 us: shifted(): return lax.ppermute(shard, axis, pairs)]
    ppermute x8 -> x0, starting transfers between devices: 37.6 us -> none  [the longest x2 23.3 us: extended_2(): before = lax.ppermute(last, axis, up)]
    all_to_all x1 -> x0, waiting for transfers between devices: 6.86 us -> none  [per_device(): lax.all_to_all(spread, ('band', 'rows'), split_axis=0, concat_axis=2, til...]
    all_to_all x1 -> x0, starting transfers between devices: 6.33 us -> none  [per_device(): lax.all_to_all(spread, ('band', 'rows'), split_axis=0, concat_axis=2, til...]
    scatter x1 -> x0, local copies, waits for them, and re-layouts: 6.29 us -> none  [per_device(): outgoing = jnp.zeros((band_total * FCAP * span_cells, channels), latents....]
    conv_general_dilated x7 -> x0, local copies, waits for them, and re-layouts: 5.5 us -> none  [convolve(): lax.conv_general_dilated(frames[None], kernel, (1, 1, 1), [(0, 0), (0, 0)...]
  transfers between devices with their start and end apart: 9 -> 0, of which waited for: 4 -> 0; matrix products, arithmetic and copies ran while one was open for 2% -> 0% of each run, Pallas kernels for 0% -> 0%
where the time goes in v1:
time: 67 us; the launch traced here: 66.7 us
  Pallas kernels  61.1 us (91%)
  local copies, waits for them, and re-layouts  4.88 us (7%)
  other arithmetic  0.76 us (1%)
    pallas_call x1, Pallas kernels, per_device(): pl.pallas_call(functools.partial(conv_kernel, bands, rows), out_shape=jax...  42.6 us
    pallas_call x1, Pallas kernels, per_device(): pl.pallas_call(functools.partial(exchange_kernel, bands, rows), out_shape...  18.5 us
    unnamed x5, local copies, waits for them, and re-layouts  2.36 us

profile of v1, /device:TPU:11, one launch (start us, length us, event | category | flops | bytes accessed | tf_op | source)
XLA Modules:
  0.0 66.7 jit_solution(2770105120945273345)
XLA Ops:
  0.0 1.2 %reshape.17.b1 = f32[1,384]{1,0:T(1,128)} reshape(f32[384]{0:T(512)} %param.11) | data formatting | bytes 3072 | tf_op jit(solution)/shard_map/reshape | solution.py:297
  1.2 0.8 %pad_maximum_fusion = f32[768]{0:T(1024)S(1)} fusion(f32[384]{0:T(512)} %param.13), kind=kLoop, calls=%fused_computation | loop fusion | flops 768 | bytes 4608 | tf_op jit(solution)/shard_map/concatenate | solution.py:299
  2.0 0.6 reshape.19.b2
  2.6 0.7 %reshape.15.cell = s32[1,1040]{1,0:T(1,128)S(1)} reshape(s32[1040]{0:T(1024)} %param.8) | data formatting | bytes 8320 | tf_op jit(solution)/shard_map/reshape | solution.py:274
  3.3 0.9 %copy.8.lat = bf16[1040,16]{1,0:T(8,128)(2,1)S(1)} copy(bf16[1040,16]{0,1:T(8,128)(2,1)} %param.7) | data formatting | bytes 66560 | tf_op args[0]
  4.2 0.0 copy-start.1
  4.2 0.6 copy-done.1
  4.9 18.5 %exchange.1.xin = bf16[8,8,16,256]{3,2,1,0:T(8,128)(2,1)S(1)} custom-call(s32[8]{0:T(128)S(1)} %copy-done.1, bf16[1040,16]{1,0:T(8,128)(2,1)S(1)} %copy.8.lat, s32[1,1040]{1,0:T(1,128)S(1)} %reshape.15.cell), custom_call_target="tpu_custom_call" | custom-call | tf_op jit(solution)/shard_map/exchange/pallas_call | solution.py:258
  23.4 0.0 copy-start
  23.4 0.8 %copy-done = bf16[8,8,16,256]{3,2,1,0:T(8,128)(2,1)} copy-done((bf16[8,8,16,256]{3,2,1,0:T(8,128)(2,1)}, bf16[8,8,16,256]{3,2,1,0:T(8,128)(2,1)S(1)}, u32[]{:S(2)}) %copy-start) | copy-done | bytes 524312
  24.2 42.6 %convs.1 = bf16[4,4,160,384]{3,2,1,0:T(8,128)(2,1)} custom-call(s32[8]{0:T(128)} %counts.3, bf16[8,8,16,256]{3,2,1,0:T(8,128)(2,1)} %copy-done, bf16[432,384]{1,0:T(8,128)(2,1)} %bitcast.3, f32[1,384]{1,0:T(1,128)} %reshape.17.b1, bf16[3,3,1152,384]{3,2,1,0:T(8,128)(2,1)} %bitcast.2, f32[1,768]{1,0:T(1,128)} %reshape.19.b2), custom_call_target="tpu_custom_call" | custom-call | flops 20384317440 | bytes 12582912 | tf_op jit(solution)/shard_map/convs/pallas_call | solution.py:276
Async XLA Ops:
  4.2 0.7 copy-start.1
  23.4 0.8 %copy-start = (bf16[8,8,16,256]{3,2,1,0:T(8,128)(2,1)}, bf16[8,8,16,256]{3,2,1,0:T(8,128)(2,1)S(1)}, u32[]{:S(2)}) copy-start(bf16[8,8,16,256]{3,2,1,0:T(8,128)(2,1)S(1)} %exchange.1.xin) | copy-start | bytes 1572868

commit v2 on v1

--- a/solution.py
+++ b/solution.py
@@ -19,8 +19,17 @@
 MESH = pl.DeviceIdType.MESH
 
 
-def exchange_kernel(bands, rows, counts, lat, cell, out, store, send, recv, send_sem, recv_sem):
-    n, channels = lat.shape
+def exchange_kernel(
+    bands, rows, counts_in, lat_in, cell_in, out,
+    counts, lat, cell, store, send, recv, send_sem, recv_sem, load_sem,
+):
+    loads = [
+        pltpu.make_async_copy(a, b, load_sem.at[i])
+        for i, (a, b) in enumerate(((cell_in, cell), (lat_in, lat), (counts_in, counts)))
+    ]
+    for load in loads:
+        load.start()
+    channels, n = lat.shape
     span = R * W // bands
     parts = W // span
     frames = n // span
@@ -52,19 +61,16 @@
         def _():
             pl.semaphore_signal(barrier, inc=1, device_id=(src_band, src_row), device_id_type=MESH)
 
-    cells = cell[...]
+    for load in loads:
+        load.wait()
+    cells = cell[...].reshape(1, n)
     frame = jnp.zeros_like(cells)
     for f in range(1, frames):
         frame = frame + (cells >= f * plane).astype(jnp.int32)
     lane_of = cells - frame * plane - me * span + part * span + 1
     lane_of = jnp.where(lane_of >= LANES, lane_of - LANES, lane_of)
-    eye = (
-        lax.broadcasted_iota(jnp.int32, (channels, channels), 0)
-        == lax.broadcasted_iota(jnp.int32, (channels, channels), 1)
-    )
-    eye = jnp.where(eye, 1.0, 0.0).astype(jnp.bfloat16)
+    lat_t = lat[...].astype(jnp.float32)
     across = (((1,), (1,)), ((), ()))
-    lat_t = lax.dot_general(eye, lat[...], across, preferred_element_type=jnp.float32)
     by_frame = jnp.concatenate(
         [jnp.where(frame == f, lat_t, 0.0).astype(jnp.bfloat16) for f in range(frames)], axis=0
     )
@@ -153,7 +159,16 @@
                 copy_to(i, target, which, slot).wait_send()
 
 
-def conv_kernel(bands, rows, counts, xin, w1, b1, w2, b2, out, xs, mid, wcat, acc, obuf, w_sem, o_sem):
+def conv_kernel(
+    bands, rows, counts_in, xin, w1_in, b1_in, w2, b2_in, out,
+    counts, w1, b1, b2, xs, mid, wcat, acc, obuf, load_sem, w_sem, o_sem,
+):
+    loads = [
+        pltpu.make_async_copy(a, b, load_sem.at[i])
+        for i, (a, b) in enumerate(((counts_in, counts), (w1_in, w1), (b1_in, b1), (b2_in, b2)))
+    ]
+    for load in loads:
+        load.start()
     channels = xin.shape[2]
     wide = w1.shape[1]
     depth = 3 * wide
@@ -168,11 +183,6 @@
     for b in range(3):
         for a in range(3):
             weight_copy(a, b).start()
-
-    start = jnp.int32(0)
-    for q in range(bands - 1):
-        start = start + jnp.where(q < band, counts[q], 0)
-    own = counts[band]
 
     def shift_row(yy, carry):
         whole = xin[yy].astype(jnp.float32)
@@ -185,36 +195,48 @@
 
     lax.fori_loop(0, IN_ROWS, shift_row, 0)
 
-    place = lax.broadcasted_iota(jnp.int32, (W, wide), 0)
-
-    def first(i, carry):
-        f = lax.div(i, MID_ROWS)
-        y = lax.rem(i, MID_ROWS)
-        taps = [xs[e, y + b, f + a] for a in range(3) for b in range(3) for e in range(3)]
-        lhs = jnp.concatenate(taps, axis=0)
-        v = lax.dot_general(
-            lhs, w1[...], (((0,), (0,)), ((), ())), preferred_element_type=jnp.float32
-        )
-        v = v + b1[...]
-        at = R * row - 1 + y
-        inside = (at >= 0) & (at < R * rows) & (start - BACK + f >= 0)
-        half = 0.5 * v
-        active = jnp.where(inside, half * jnp.tanh(half) + half, 0.0)
-        before = jnp.where(place == 0, 0.0, pltpu.roll(active, 1, 0))
-        after = jnp.where(place == W - 1, 0.0, pltpu.roll(active, W - 1, 0))
-        mid[f, y, :, :wide] = before.astype(jnp.bfloat16)
-        mid[f, y, :, wide:2 * wide] = active.astype(jnp.bfloat16)
-        mid[f, y, :, 2 * wide:] = after.astype(jnp.bfloat16)
+    for load in loads:
+        load.wait()
+    start = jnp.int32(0)
+    for q in range(bands - 1):
+        start = start + jnp.where(q < band, counts[q], 0)
+    own = counts[band]
+
+    place = lax.broadcasted_iota(jnp.int32, (8, wide), 0)
+    bias1 = b1[...].reshape(1, wide)
+
+    def first(f, carry):
+        for y in range(MID_ROWS):
+            taps = [xs[e, y + b, f + a] for a in range(3) for b in range(3) for e in range(3)]
+            v = lax.dot_general(
+                jnp.concatenate(taps, axis=0),
+                w1[...],
+                (((0,), (0,)), ((), ())),
+                preferred_element_type=jnp.float32,
+            )
+            at = R * row - 1 + y
+            inside = (at >= 0) & (at < R * rows) & (start - BACK + f >= 0)
+            half = (v + bias1) * jnp.where(inside, 0.5, 0.0)
+            active = half * jnp.tanh(half) + half
+            before = pltpu.roll(active, 1, 0)
+            before = jnp.concatenate([jnp.where(place == 0, 0.0, before[:8]), before[8:]], axis=0)
+            after = pltpu.roll(active, W - 1, 0)
+            after = jnp.concatenate([after[:-8], jnp.where(place == 7, 0.0, after[-8:])], axis=0)
+            mid[f, y, :, :wide] = before.astype(jnp.bfloat16)
+            mid[f, y, :, wide:2 * wide] = active.astype(jnp.bfloat16)
+            mid[f, y, :, 2 * wide:] = after.astype(jnp.bfloat16)
         return carry
 
-    lax.fori_loop(0, MID_FRAMES * MID_ROWS, first, 0)
+    lax.fori_loop(0, MID_FRAMES, first, 0)
 
     for b in range(3):
         for a in range(3):
             weight_copy(a, b).wait()
 
     for pair in range(FCAP // 2):
-        acc[...] = jnp.broadcast_to(b2[...], acc.shape)
+        bias = jnp.broadcast_to(b2[...].reshape(1, wide), (R * W, wide))
+        acc[:, :wide] = bias
+        acc[:, wide:] = bias
 
         def taps_of(b, carry):
             def rows_of(g):
@@ -252,51 +274,59 @@
     parts = W // span
     frames = n // span
     vmem = pl.BlockSpec(memory_space=pltpu.VMEM)
-    smem = pl.BlockSpec(memory_space=pltpu.SMEM)
-    anywhere = pl.BlockSpec(memory_space=pl.ANY)
+    hbm = pl.BlockSpec(memory_space=pltpu.HBM)
     tile = (IN_FRAMES, channels, LANES)
     xin = pl.pallas_call(
         functools.partial(exchange_kernel, bands, rows),
         out_shape=jax.ShapeDtypeStruct((IN_ROWS, IN_FRAMES, channels, 2 * LANES), jnp.bfloat16),
-        in_specs=[smem, vmem, vmem],
+        in_specs=[hbm] * 3,
         out_specs=vmem,
         scratch_shapes=[
+            pltpu.SMEM((bands,), jnp.int32),
+            pltpu.VMEM((channels, n), jnp.bfloat16),
+            pltpu.VMEM((n,), jnp.int32),
             pltpu.VMEM((frames + 2 * FCAP, channels, LANES), jnp.bfloat16),
             pltpu.VMEM((bands,) + tile, jnp.bfloat16),
             pltpu.VMEM((IN_ROWS * parts,) + tile, jnp.bfloat16),
             pltpu.SemaphoreType.DMA((2, bands)),
             pltpu.SemaphoreType.DMA((IN_ROWS * parts,)),
+            pltpu.SemaphoreType.DMA((3,)),
         ],
         compiler_params=pltpu.CompilerParams(
-            collective_id=0, has_side_effects=True, vmem_limit_bytes=32 * 1024 * 1024
+            collective_id=0, has_side_effects=True, vmem_limit_bytes=60 * 1024 * 1024
         ),
         name="exchange",
-    )(frame_counts, latents, token_cell.reshape(1, n))
+    )(frame_counts, latents.T, token_cell)
     flops = 2 * FCAP * R * W * 27 * wide * wide
     return pl.pallas_call(
         functools.partial(conv_kernel, bands, rows),
         out_shape=jax.ShapeDtypeStruct((FCAP, R, W, wide), jnp.bfloat16),
-        in_specs=[smem, vmem, vmem, vmem, anywhere, vmem],
-        out_specs=anywhere,
+        in_specs=[hbm, vmem, hbm, hbm, hbm, hbm],
+        out_specs=hbm,
         scratch_shapes=[
+            pltpu.SMEM((bands,), jnp.int32),
+            pltpu.VMEM((27 * channels, wide), jnp.bfloat16),
+            pltpu.VMEM((wide,), jnp.float32),
+            pltpu.VMEM((wide,), jnp.float32),
             pltpu.VMEM((3, IN_ROWS, IN_FRAMES, channels, W), jnp.bfloat16),
             pltpu.VMEM((MID_FRAMES, MID_ROWS, W, 3 * wide), jnp.bfloat16),
             pltpu.VMEM((3, 3 * wide, 3 * wide), jnp.bfloat16),
             pltpu.VMEM((R * W, 2 * wide), jnp.float32),
             pltpu.VMEM((FCAP, R, W, wide), jnp.bfloat16),
+            pltpu.SemaphoreType.DMA((4,)),
             pltpu.SemaphoreType.DMA((3, 3)),
             pltpu.SemaphoreType.DMA((FCAP,)),
         ],
-        compiler_params=pltpu.CompilerParams(vmem_limit_bytes=56 * 1024 * 1024),
+        compiler_params=pltpu.CompilerParams(vmem_limit_bytes=60 * 1024 * 1024),
         cost_estimate=pl.CostEstimate(flops=flops, bytes_accessed=12 << 20, transcendentals=0),
         name="convs",
     )(
         frame_counts,
         xin,
         in_kernel.reshape(27 * channels, wide),
-        in_bias.reshape(1, wide),
+        in_bias,
         mid_kernel.reshape(3, 3, 3 * wide, wide),
-        jnp.concatenate([mid_bias, mid_bias]).reshape(1, 2 * wide),
+        mid_bias,
     )
 
 

time: 67 us -> 55.8 us (0.83)
  Pallas kernels: 61.1 us -> 55.6 us
  local copies, waits for them, and re-layouts: 4.88 us -> 0 us
  other arithmetic: 0.76 us -> 0 us
    pallas_call x1, Pallas kernels: 42.6 us -> 36.9 us  [per_device(): pl.pallas_call(functools.partial(conv_kernel, bands, rows), out_shape=jax...]
    reshape x3 -> x0, local copies, waits for them, and re-layouts: 2.52 us -> none  [the longest x1 1.22 us: per_device(): in_bias.reshape(1, wide)]
    unnamed x5 -> x0, local copies, waits for them, and re-layouts: 2.36 us -> none
    concatenate x1 -> x0, other arithmetic: 0.76 us -> none  [per_device(): jnp.concatenate([mid_bias, mid_bias]).reshape(1, 2 * wide)]
where the time goes in v2:
time: 55.8 us; the launch traced here: 55.6 us
  Pallas kernels  55.6 us (100%)
    pallas_call x1, Pallas kernels, per_device(): pl.pallas_call(functools.partial(conv_kernel, bands, rows), out_shape=jax...  36.9 us
    pallas_call x1, Pallas kernels, per_device(): pl.pallas_call(functools.partial(exchange_kernel, bands, rows), out_shape...  18.7 us

profile of v2, /device:TPU:11, one launch (start us, length us, event | category | flops | bytes accessed | tf_op | source)
XLA Modules:
  0.0 55.6 jit_solution(15219594477864213892)
XLA Ops:
  0.0 18.7 %exchange.1.xin = bf16[8,8,16,256]{3,2,1,0:T(8,128)(2,1)} custom-call(s32[8]{0:T(128)} %counts_in.3, bf16[16,1040]{1,0:T(8,128)(2,1)} %bitcast.3, s32[1040]{0:T(1024)} %cell_in.1), custom_call_target="tpu_custom_call" | custom-call | tf_op jit(solution)/shard_map/exchange/pallas_call | solution.py:279
  18.7 36.9 %convs.1 = bf16[4,4,160,384]{3,2,1,0:T(8,128)(2,1)} custom-call(s32[8]{0:T(128)} %counts_in.3, bf16[8,8,16,256]{3,2,1,0:T(8,128)(2,1)} %exchange.1.xin, bf16[432,384]{1,0:T(8,128)(2,1)} %bitcast.5, f32[384]{0:T(512)} %b1_in.1, bf16[3,3,1152,384]{3,2,1,0:T(8,128)(2,1)} %bitcast.4, f32[384]{0:T(512)} %b2_in.1), custom_call_target="tpu_custom_call" | custom-call | flops 20384317440 | bytes 12582912 | tf_op jit(solution)/shard_map/convs/pallas_call | solution.py:301

commit v3 on v2

--- a/solution.py
+++ b/solution.py
@@ -161,7 +161,7 @@
 
 def conv_kernel(
     bands, rows, counts_in, xin, w1_in, b1_in, w2, b2_in, out,
-    counts, w1, b1, b2, xs, mid, wcat, acc, obuf, load_sem, w_sem, o_sem,
+    counts, w1, b1, b2, xl, w1p, mid, wcat, acc, obuf, load_sem, w_sem, o_sem,
 ):
     loads = [
         pltpu.make_async_copy(a, b, load_sem.at[i])
@@ -184,16 +184,22 @@
         for a in range(3):
             weight_copy(a, b).start()
 
-    def shift_row(yy, carry):
-        whole = xin[yy].astype(jnp.float32)
-        flat = whole.reshape(IN_FRAMES * channels, 2 * LANES)
-        for e in range(3):
-            moved = flat if e == 0 else pltpu.roll(flat, 2 * LANES - e, 1)
-            moved = moved[:, :W].astype(jnp.bfloat16)
-            xs[e, yy] = moved.reshape(IN_FRAMES, channels, W)
+    half_lane = lax.broadcasted_iota(jnp.int32, (W, LANES), 1) < LANES // 2
+
+    def spread_row(yy, carry):
+        flat = xin[yy].astype(jnp.float32).reshape(IN_FRAMES * channels, 2 * LANES)
+        turned = flat.T
+        rolled = {k: turned if k == 0 else pltpu.roll(turned, k, 1) for k in (0, 32, 64, 96)}
+        for p in range(MID_FRAMES // 2):
+            even = rolled[(LANES - 32 * p) % LANES]
+            odd = rolled[(LANES + 64 - 32 * p) % LANES]
+            low = jnp.where(half_lane, even[:W], odd[1:W + 1])
+            high = jnp.where(half_lane, even[2:W + 2], 0.0)
+            xl[p, yy, :, :LANES] = low.astype(jnp.bfloat16)
+            xl[p, yy, :, LANES:] = high.astype(jnp.bfloat16)
         return carry
 
-    lax.fori_loop(0, IN_ROWS, shift_row, 0)
+    lax.fori_loop(0, IN_ROWS, spread_row, 0)
 
     for load in loads:
         load.wait()
@@ -205,29 +211,38 @@
     place = lax.broadcasted_iota(jnp.int32, (8, wide), 0)
     bias1 = b1[...].reshape(1, wide)
 
-    def first(f, carry):
+    w1p[...] = jnp.zeros(w1p.shape, jnp.bfloat16)
+    for a in range(3):
+        for b in range(3):
+            for e in range(3):
+                tap = w1[pl.ds(((a * 3 + b) * 3 + e) * channels, channels), :]
+                for k in range(2):
+                    to = b * 2 * LANES + e * (LANES // 2) + (k + a) * channels
+                    w1p[to:to + channels, k * wide:(k + 1) * wide] = tap
+
+    def first(p, carry):
         for y in range(MID_ROWS):
-            taps = [xs[e, y + b, f + a] for a in range(3) for b in range(3) for e in range(3)]
-            v = lax.dot_general(
-                jnp.concatenate(taps, axis=0),
-                w1[...],
-                (((0,), (0,)), ((), ())),
-                preferred_element_type=jnp.float32,
-            )
-            at = R * row - 1 + y
-            inside = (at >= 0) & (at < R * rows) & (start - BACK + f >= 0)
-            half = (v + bias1) * jnp.where(inside, 0.5, 0.0)
-            active = half * jnp.tanh(half) + half
-            before = pltpu.roll(active, 1, 0)
-            before = jnp.concatenate([jnp.where(place == 0, 0.0, before[:8]), before[8:]], axis=0)
-            after = pltpu.roll(active, W - 1, 0)
-            after = jnp.concatenate([after[:-8], jnp.where(place == 7, 0.0, after[-8:])], axis=0)
-            mid[f, y, :, :wide] = before.astype(jnp.bfloat16)
-            mid[f, y, :, wide:2 * wide] = active.astype(jnp.bfloat16)
-            mid[f, y, :, 2 * wide:] = after.astype(jnp.bfloat16)
+            lhs = jnp.concatenate([xl[p, y + b] for b in range(3)], axis=1)
+            both = jnp.dot(lhs, w1p[...], preferred_element_type=jnp.float32)
+            for k in range(2):
+                f = 2 * p + k
+                finish(f, y, both[:, k * wide:(k + 1) * wide])
         return carry
 
-    lax.fori_loop(0, MID_FRAMES, first, 0)
+    def finish(f, y, v):
+        at = R * row - 1 + y
+        inside = (at >= 0) & (at < R * rows) & (start - BACK + f >= 0)
+        half = (v + bias1) * jnp.where(inside, 0.5, 0.0)
+        active = half * jnp.tanh(half) + half
+        before = pltpu.roll(active, 1, 0)
+        before = jnp.concatenate([jnp.where(place == 0, 0.0, before[:8]), before[8:]], axis=0)
+        after = pltpu.roll(active, W - 1, 0)
+        after = jnp.concatenate([after[:-8], jnp.where(place == 7, 0.0, after[-8:])], axis=0)
+        mid[f, y, :, :wide] = before.astype(jnp.bfloat16)
+        mid[f, y, :, wide:2 * wide] = active.astype(jnp.bfloat16)
+        mid[f, y, :, 2 * wide:] = after.astype(jnp.bfloat16)
+
+    lax.fori_loop(0, MID_FRAMES // 2, first, 0)
 
     for b in range(3):
         for a in range(3):
@@ -308,7 +323,8 @@
             pltpu.VMEM((27 * channels, wide), jnp.bfloat16),
             pltpu.VMEM((wide,), jnp.float32),
             pltpu.VMEM((wide,), jnp.float32),
-            pltpu.VMEM((3, IN_ROWS, IN_FRAMES, channels, W), jnp.bfloat16),
+            pltpu.VMEM((MID_FRAMES // 2, IN_ROWS, W, 2 * LANES), jnp.bfloat16),
+            pltpu.VMEM((6 * LANES, 2 * wide), jnp.bfloat16),
             pltpu.VMEM((MID_FRAMES, MID_ROWS, W, 3 * wide), jnp.bfloat16),
             pltpu.VMEM((3, 3 * wide, 3 * wide), jnp.bfloat16),
             pltpu.VMEM((R * W, 2 * wide), jnp.float32),

time: 55.8 us -> 55.4 us (level)
  no operation moved by 1% of the time
where the time goes in v3:
time: 55.4 us; the launch traced here: 55.2 us
  Pallas kernels  55.2 us (100%)
    pallas_call x1, Pallas kernels, per_device(): pl.pallas_call(functools.partial(conv_kernel, bands, rows), out_shape=jax...  36.5 us
    pallas_call x1, Pallas kernels, per_device(): pl.pallas_call(functools.partial(exchange_kernel, bands, rows), out_shape...  18.7 us

profile of v3, /device:TPU:11, one launch (start us, length us, event | category | flops | bytes accessed | tf_op | source)
XLA Modules:
  0.0 55.2 jit_solution(4960690189386269088)
XLA Ops:
  0.0 18.7 %exchange.1.xin = bf16[8,8,16,256]{3,2,1,0:T(8,128)(2,1)} custom-call(s32[8]{0:T(128)} %counts_in.3, bf16[16,1040]{1,0:T(8,128)(2,1)} %bitcast.3, s32[1040]{0:T(1024)} %cell_in.1), custom_call_target="tpu_custom_call" | custom-call | tf_op jit(solution)/shard_map/exchange/pallas_call | solution.py:294
  18.7 36.5 %convs.1 = bf16[4,4,160,384]{3,2,1,0:T(8,128)(2,1)} custom-call(s32[8]{0:T(128)} %counts_in.3, bf16[8,8,16,256]{3,2,1,0:T(8,128)(2,1)} %exchange.1.xin, bf16[432,384]{1,0:T(8,128)(2,1)} %bitcast.5, f32[384]{0:T(512)} %b1_in.1, bf16[3,3,1152,384]{3,2,1,0:T(8,128)(2,1)} %bitcast.4, f32[384]{0:T(512)} %b2_in.1), custom_call_target="tpu_custom_call" | custom-call | flops 20384317440 | bytes 12582912 | tf_op jit(solution)/shard_map/convs/pallas_call | solution.py:316

commit v4 on v3

--- a/solution.py
+++ b/solution.py
@@ -67,8 +67,7 @@
     frame = jnp.zeros_like(cells)
     for f in range(1, frames):
         frame = frame + (cells >= f * plane).astype(jnp.int32)
-    lane_of = cells - frame * plane - me * span + part * span + 1
-    lane_of = jnp.where(lane_of >= LANES, lane_of - LANES, lane_of)
+    lane_of = cells - frame * plane - me * span
     lat_t = lat[...].astype(jnp.float32)
     across = (((1,), (1,)), ((), ()))
     by_frame = jnp.concatenate(
@@ -85,6 +84,9 @@
     total = bands + jnp.where(near_ok, bands, 0) - here
     pl.semaphore_wait(barrier, total)
 
+    packed = send.shape[2]
+    lane = lax.broadcasted_iota(jnp.int32, (channels, LANES), 1)
+
     def copy_to(i, target, which, slot):
         to_band = lax.rem(band + i, bands)
         return pltpu.make_async_remote_copy(
@@ -101,8 +103,15 @@
         start = jnp.int32(0)
         for q in range(bands - 1):
             start = start + jnp.where(q < to_band, counts[q], 0)
+        tiles = [jnp.zeros((channels, LANES), jnp.float32)] * (packed // LANES)
         for j in range(IN_FRAMES):
-            send[i, j] = store[start + j]
+            m, by = divmod(span * j, LANES)
+            piece = store[start + j].astype(jnp.float32)
+            piece = pltpu.roll(piece, by, 1) if by else piece
+            if by + span > LANES:
+                tiles[m + 1] = jnp.where(lane < by, piece, tiles[m + 1])
+            tiles[m] = jnp.where(lane >= by, piece, tiles[m]) if by else piece
+        send[i] = jnp.concatenate(tiles, axis=1).astype(jnp.bfloat16)
         for which, target, slot, ok in ((0, home, slot_home, None), (1, near, slot_near, near_ok)):
             away = jnp.bool_(True) if i else target != row
             go = away if ok is None else away & ok
@@ -130,20 +139,28 @@
                 device_id_type=MESH,
             ).wait_recv()
 
-    lane = lax.broadcasted_iota(jnp.int32, (IN_FRAMES, channels, LANES), 2)
     for yy in range(IN_ROWS):
         at = R * row - 2 + yy
         inside = (at >= 0) & (at < R * rows)
 
         @pl.when(inside)
         def _():
-            low = recv[yy * parts].astype(jnp.float32)
-            for p in range(1, parts):
-                piece = recv[yy * parts + p].astype(jnp.float32)
-                low = jnp.where(lane >= p * span + 1, piece, low)
-            high = jnp.where(lane < W + 1 - LANES, piece, 0.0)
-            out[yy, :, :, :LANES] = low.astype(jnp.bfloat16)
-            out[yy, :, :, LANES:] = high.astype(jnp.bfloat16)
+            rows_in = [recv[yy * parts + p].astype(jnp.float32) for p in range(parts)]
+            for j in range(IN_FRAMES):
+                m, by = divmod(span * j, LANES)
+                low = jnp.zeros((channels, LANES), jnp.float32)
+                for p in range(parts):
+                    piece = rows_in[p][:, m * LANES:(m + 1) * LANES]
+                    if by + span > LANES:
+                        over = rows_in[p][:, (m + 1) * LANES:(m + 2) * LANES]
+                        piece = jnp.where(lane >= by, piece, over)
+                    to = p * span + 1
+                    turn = (to - by) % LANES
+                    piece = pltpu.roll(piece, turn, 1) if turn else piece
+                    low = jnp.where(lane >= to, piece, low)
+                high = jnp.where(lane < W + 1 - LANES, piece, 0.0)
+                out[yy, j, :, :LANES] = low.astype(jnp.bfloat16)
+                out[yy, j, :, LANES:] = high.astype(jnp.bfloat16)
 
         @pl.when(jnp.logical_not(inside))
         def _():
@@ -177,7 +194,7 @@
 
     def weight_copy(a, b):
         return pltpu.make_async_copy(
-            w2.at[a, b], wcat.at[b, :, pl.ds((2 - a) * wide, wide)], w_sem.at[a, b]
+            w2.at[a, b], wcat.at[pl.ds(b * depth, depth), pl.ds((2 - a) * wide, wide)], w_sem.at[a, b]
         )
 
     for b in range(3):
@@ -238,9 +255,11 @@
         before = jnp.concatenate([jnp.where(place == 0, 0.0, before[:8]), before[8:]], axis=0)
         after = pltpu.roll(active, W - 1, 0)
         after = jnp.concatenate([after[:-8], jnp.where(place == 7, 0.0, after[-8:])], axis=0)
-        mid[f, y, :, :wide] = before.astype(jnp.bfloat16)
-        mid[f, y, :, wide:2 * wide] = active.astype(jnp.bfloat16)
-        mid[f, y, :, 2 * wide:] = after.astype(jnp.bfloat16)
+        for e, tap in enumerate((before, active, after)):
+            tap = tap.astype(jnp.bfloat16)
+            for b in range(max(0, y - R + 1), min(3, y + 1)):
+                at_lane = b * depth + e * wide
+                mid[f, y - b, :, at_lane:at_lane + wide] = tap
 
     lax.fori_loop(0, MID_FRAMES // 2, first, 0)
 
@@ -248,36 +267,25 @@
         for a in range(3):
             weight_copy(a, b).wait()
 
-    for pair in range(FCAP // 2):
-        bias = jnp.broadcast_to(b2[...].reshape(1, wide), (R * W, wide))
-        acc[:, :wide] = bias
-        acc[:, wide:] = bias
-
-        def taps_of(b, carry):
-            def rows_of(g):
-                return mid[2 * pair + g, pl.ds(b, R)].reshape(R * W, depth)
-
-            acc[:, :wide] += jnp.dot(
-                rows_of(0), wcat[b, :, 2 * wide:], preferred_element_type=jnp.float32
-            )
-            acc[...] += jnp.dot(
-                rows_of(1), wcat[b, :, wide:], preferred_element_type=jnp.float32
-            )
-            acc[...] += jnp.dot(
-                rows_of(2), wcat[b, :, :2 * wide], preferred_element_type=jnp.float32
-            )
-            acc[:, wide:] += jnp.dot(
-                rows_of(3), wcat[b, :, :wide], preferred_element_type=jnp.float32
-            )
-            return carry
-
-        lax.fori_loop(0, 3, taps_of, 0)
-        for k in range(2):
+    bias2 = b2[...].reshape(1, wide)
+
+    def mix(pair, carry):
+        def product(g, first_tap, last_tap):
+            lhs = mid[2 * pair + g].reshape(R * W, 3 * depth)
+            rhs = wcat[:, first_tap * wide:last_tap * wide]
+            return jnp.dot(lhs, rhs, preferred_element_type=jnp.float32)
+
+        acc[...] = product(1, 1, 3)
+        acc[...] += product(2, 0, 2)
+        for k, g, tap in ((0, 0, 2), (1, 3, 0)):
             t = 2 * pair + k
-            value = acc[:, k * wide:(k + 1) * wide]
+            value = acc[:, k * wide:(k + 1) * wide] + product(g, tap, tap + 1) + bias2
             value = jnp.where(t < own, value, 0.0).astype(jnp.bfloat16)
             obuf[t] = value.reshape(R, W, wide)
             pltpu.make_async_copy(obuf.at[t], out.at[t], o_sem.at[t]).start()
+        return carry
+
+    lax.fori_loop(0, FCAP // 2, mix, 0)
     for t in range(FCAP):
         pltpu.make_async_copy(obuf.at[t], out.at[t], o_sem.at[t]).wait()
 
@@ -290,7 +298,7 @@
     frames = n // span
     vmem = pl.BlockSpec(memory_space=pltpu.VMEM)
     hbm = pl.BlockSpec(memory_space=pltpu.HBM)
-    tile = (IN_FRAMES, channels, LANES)
+    tile = (channels, -(-IN_FRAMES * span // LANES) * LANES)
     xin = pl.pallas_call(
         functools.partial(exchange_kernel, bands, rows),
         out_shape=jax.ShapeDtypeStruct((IN_ROWS, IN_FRAMES, channels, 2 * LANES), jnp.bfloat16),
@@ -325,8 +333,8 @@
             pltpu.VMEM((wide,), jnp.float32),
             pltpu.VMEM((MID_FRAMES // 2, IN_ROWS, W, 2 * LANES), jnp.bfloat16),
             pltpu.VMEM((6 * LANES, 2 * wide), jnp.bfloat16),
-            pltpu.VMEM((MID_FRAMES, MID_ROWS, W, 3 * wide), jnp.bfloat16),
-            pltpu.VMEM((3, 3 * wide, 3 * wide), jnp.bfloat16),
+            pltpu.VMEM((MID_FRAMES, R, W, 9 * wide), jnp.bfloat16),
+            pltpu.VMEM((9 * wide, 3 * wide), jnp.bfloat16),
             pltpu.VMEM((R * W, 2 * wide), jnp.float32),
             pltpu.VMEM((FCAP, R, W, wide), jnp.bfloat16),
             pltpu.SemaphoreType.DMA((4,)),

time: 55.4 us -> 49.7 us (0.90)
  Pallas kernels: 55.2 us -> 49.5 us
    pallas_call x1, Pallas kernels: 18.7 us -> 15.3 us  [per_device(): pl.pallas_call(functools.partial(exchange_kernel, bands, rows), out_shape...]
    pallas_call x1, Pallas kernels: 36.5 us -> 34.2 us  [per_device(): pl.pallas_call(functools.partial(conv_kernel, bands, rows), out_shape=jax...]
where the time goes in v4:
time: 49.7 us; the launch traced here: 49.5 us
  Pallas kernels  49.5 us (100%)
    pallas_call x1, Pallas kernels, per_device(): pl.pallas_call(functools.partial(conv_kernel, bands, rows), out_shape=jax...  34.2 us
    pallas_call x1, Pallas kernels, per_device(): pl.pallas_call(functools.partial(exchange_kernel, bands, rows), out_shape...  15.3 us

profile of v4, /device:TPU:11, one launch (start us, length us, event | category | flops | bytes accessed | tf_op | source)
XLA Modules:
  0.0 49.5 jit_solution(4053923332041299776)
XLA Ops:
  0.0 15.3 %exchange.1.xin = bf16[8,8,16,256]{3,2,1,0:T(8,128)(2,1)} custom-call(s32[8]{0:T(128)} %counts_in.3, bf16[16,1040]{1,0:T(8,128)(2,1)} %bitcast.3, s32[1040]{0:T(1024)} %cell_in.1), custom_call_target="tpu_custom_call" | custom-call | tf_op jit(solution)/shard_map/exchange/pallas_call | solution.py:302
  15.3 34.2 %convs.1 = bf16[4,4,160,384]{3,2,1,0:T(8,128)(2,1)} custom-call(s32[8]{0:T(128)} %counts_in.3, bf16[8,8,16,256]{3,2,1,0:T(8,128)(2,1)} %exchange.1.xin, bf16[432,384]{1,0:T(8,128)(2,1)} %bitcast.5, f32[384]{0:T(512)} %b1_in.1, bf16[3,3,1152,384]{3,2,1,0:T(8,128)(2,1)} %bitcast.4, f32[384]{0:T(512)} %b2_in.1), custom_call_target="tpu_custom_call" | custom-call | flops 20384317440 | bytes 12582912 | tf_op jit(solution)/shard_map/convs/pallas_call | solution.py:324
